TPU v7x, 1024 devices: a whole 4x4x32 slice. The times are simulated.
1024 devices in a mesh: grp: 32 (over z), dev: 32 (over y, x, core).
Axes of the slice: x: 4, y: 4, z: 32, core: 2. Of those that a mesh axis runs over, the one named last changes fastest.
Arguments:
- basis: float32 [64, 131072], P(None, ('grp', 'dev')), may hold values from -6 to 6
- own_tiles: bfloat16 [1024, 32, 128, 128], P(('grp', 'dev')), may hold values from -0.0625 to 0.0625
- own_col: int32 [1024, 32], P(('grp', 'dev')), may hold values from 0 to 63
- help_tiles: bfloat16 [1024, 32, 2, 128, 128], P(('grp', 'dev')), may hold values from -0.0625 to 0.0625
- help_col: int32 [1024, 32, 2], P(('grp', 'dev')), may hold values from 0 to 31
- help_count: int32 [1024, 32], P(('grp', 'dev')), may hold values from 0 to 2, as said below
Outputs:
- filtered: float32 [64, 131072], P(None, ('grp', 'dev'))
- gram: float32 [64, 64], replicated
Inputs may be any that keep to these rules, and one draw needn't show every extreme that they name: `help_count`: each helper row has one row block of its group with all 2 slots live.
All inputs are finite; a program needn't handle non-finite values.
Results may differ from a plain program's by a relative error of at most 0.0034.
Values may be sent and summed in bfloat16 or wider, within the bound.
No kernel may reach another device: no remote copies, remote signals or barrier semaphores. Data moves between devices by JAX's collectives and lax.ppermute only.
A program may use at most 32 MiB of HBM per device.

v0:
```python
import functools

import jax
import jax.numpy as jnp
from jax import lax
from jax.experimental import pallas as pl
from jax.experimental.pallas import tpu as pltpu
from jax.sharding import PartitionSpec as P

STRIDE = 4
SHIFTS = {2: (1, -1), 4: (1, 2, -1)}[STRIDE]
UNROLL = 8
HEADER = 16
CUTS = 8
SHARED_VMEM = 16 * 1024 * 1024
WHOLE_VMEM = 60 * 1024 * 1024
BF16, F32, I32 = jnp.bfloat16, jnp.float32, jnp.int32


def add_tiles(total, blocks, tiles):
    return total + lax.dot_general(
        jnp.concatenate(blocks, axis=1),
        jnp.concatenate(tiles, axis=1),
        (((1,), (1,)), ((), ())),
        preferred_element_type=F32,
    )


def masked(block, live):
    return jnp.where(live, block, jnp.zeros_like(block))


def start_all(pairs, sem, first=0):
    copies = [
        pltpu.make_async_copy(source, target, sem.at[first + i])
        for i, (source, target) in enumerate(pairs)
    ]
    for copy in copies:
        copy.start()
    return copies


def cut(source, target, parts):
    step = max(1, target.shape[0] // parts)
    parts = target.shape[0] // step
    return [
        (source.at[pl.ds(i * step, step)], target.at[pl.ds(i * step, step)]) for i in range(parts)
    ]


def first_kernel(col_at, count_at, basis, help_, packed, rounded, col, count, block, copies, sem):
    group, tile_rows, tile = help_.shape
    rows, slots = basis.shape[0], col_at.shape[0]
    begun = start_all(
        [(basis, block)]
        + [(a, b) for a, b in cut(help_, copies.at[:, pl.ds(0, tile_rows)], CUTS)],
        sem,
    )
    scalars = start_all([(col_at, col), (count_at, count)], sem, 1 + 2 * CUTS)
    lane = lax.broadcasted_iota(I32, (HEADER, tile), 1)

    def fill(p, carry):
        codes = jnp.full((HEADER, tile), -1, I32)
        for s in range(slots):
            codes = jnp.where(lane == s, jnp.where(s < count[0, p], col[s, p], -1), codes)
        copies[p, pl.ds(tile_rows + rows, HEADER)] = codes.astype(F32).astype(BF16)
        return carry

    begun[0].wait()
    value = block[...].astype(BF16)
    rounded[...] = value
    copies[:, pl.ds(tile_rows, rows)] = jnp.broadcast_to(value[None], (group, rows, tile))
    for copy in scalars:
        copy.wait()
    lax.fori_loop(0, group, fill, 0)
    ended = []
    for i, pair in enumerate(cut(copies, packed, CUTS)):
        begun[1 + i].wait()
        ended += start_all([pair], sem, 1 + CUTS + i)
    for copy in ended:
        copy.wait()


def help_kernel(at, lent, blocks, packed, out):
    rows, tile = out.shape
    slots = lent.shape[1]
    total = jnp.zeros(out.shape, F32)
    for t in range(0, packed.shape[0] * slots, UNROLL):
        places = [(i // slots, i % slots) for i in range(t, t + UNROLL)]
        codes = [lent[u, s] for u, s in places]
        total = add_tiles(
            total,
            [masked(blocks[jnp.where(c >= 0, c, 0), pl.ds(at, rows)], c >= 0) for c in codes],
            [packed[u, pl.ds(s * tile, tile)] for u, s in places],
        )
    out[...] = total


def own_kernel(order, at, pieces, mine, code, blocks, *refs):
    parts, own, refs = refs[:pieces], refs[pieces], refs[pieces + 1 :]
    if order == 0:
        near, now, nxt, dev_out, grp_out = refs
    elif order == 1:
        near, now, before, nxt, dev_out, grp_out = refs
    else:
        near, now, before, nxt, gram = refs
    group, rows, total_runs = blocks.shape[0], near.shape[0], parts[0].shape[0]

    def pick(c):
        live = c >= group
        far = jnp.where(live, c - group, 0)
        turn = lax.rem(far - mine[0] + STRIDE * total_runs, STRIDE)
        run = lax.div(far, STRIDE)
        found = blocks[jnp.where(live, 0, c), pl.ds(at, rows)]
        for i in range(STRIDE):
            found = jnp.where(live & (turn == i), parts[i][run], found)
        return found

    product = near[...]
    for t in range(0, own.shape[0], UNROLL):
        codes = [code[0, i] for i in range(t, t + UNROLL)]
        product = add_tiles(
            product, [pick(c) for c in codes], [own[i] for i in range(t, t + UNROLL)]
        )
    if order == 0:
        value = (product - 0.5 * now[...]) / 1.5
    else:
        value = 2.0 * (product - 0.5 * now[...]) / 1.5 - before[...]
    nxt[...] = value
    if order < 2:
        rounded = value.astype(BF16)[None]
        dev_out[...] = jnp.broadcast_to(rounded, dev_out.shape)
        grp_out[...] = jnp.broadcast_to(rounded, grp_out.shape)
    else:
        whole = lax.dot_general(
            value,
            value,
            (((1,), (1,)), ((), ())),
            precision=lax.Precision.HIGHEST,
            preferred_element_type=F32,
        )
        n = gram.shape[0]
        rows = [whole[i : i + n] for i in range(0, whole.shape[0], n)]
        gram[...] = jnp.concatenate(rows, axis=1).reshape(gram.shape)


def sum_kernel(parts, out):
    out[...] = jnp.broadcast_to(jnp.sum(parts[...], axis=0, keepdims=True), out.shape)


def last_kernel(nodes, parts, out):
    whole = parts[...].reshape(parts.shape[0], parts.shape[2]) / nodes
    n, width = whole.shape[0], out.shape[1]
    for i in range(out.shape[0] // n):
        out[pl.ds(i * n, n)] = whole[:, i * width : (i + 1) * width]


def on_device(basis, own_tiles, own_col, help_tiles, help_col, help_count):
    width, tile = basis.shape
    group_size = lax.axis_size("dev")
    group_count = lax.axis_size("grp")
    slots = help_tiles.shape[2]
    own_n = own_tiles.shape[1]
    runs = group_count // STRIDE
    mine = lax.axis_index("grp").astype(I32)[None]
    vmem = pl.BlockSpec(memory_space=pltpu.VMEM)
    smem = pl.BlockSpec(memory_space=pltpu.SMEM)
    hbm = pl.BlockSpec(memory_space=pltpu.HBM)
    anywhere = pl.BlockSpec(memory_space=pl.ANY)
    whole = pltpu.CompilerParams(vmem_limit_bytes=WHOLE_VMEM)
    shared = pltpu.CompilerParams(vmem_limit_bytes=SHARED_VMEM)
    strided = [[b + STRIDE * a for a in range(runs)] for b in range(STRIDE)]
    block = jax.ShapeDtypeStruct((width, tile), F32)
    tile_rows = slots * tile

    packed, rounded = pl.pallas_call(
        first_kernel,
        out_shape=(
            jax.ShapeDtypeStruct((group_size, tile_rows + width + HEADER, tile), BF16),
            jax.ShapeDtypeStruct((width, tile), BF16),
        ),
        in_specs=[anywhere] * 4,
        out_specs=(hbm, vmem),
        scratch_shapes=[
            pltpu.SMEM((slots, group_size), I32),
            pltpu.SMEM((1, group_size), I32),
            pltpu.VMEM((width, tile), F32),
            pltpu.VMEM((group_size, tile_rows + width + HEADER, tile), BF16),
            pltpu.SemaphoreType.DMA((3 + 2 * CUTS,)),
        ],
        compiler_params=whole,
        name="first_copies",
    )(help_col[0].T, help_count, basis, help_tiles[0].reshape(group_size, tile_rows, tile))

    def from_neighbours(strided_blocks):
        shifted = [strided_blocks]
        for n, shift in enumerate(SHIFTS):
            piece = strided_blocks
            if STRIDE == 2:
                piece = strided_blocks[n * (runs // 2) : (n + 1) * (runs // 2)]
            turns = [shift if i % 2 or abs(shift) == 1 else -shift for i in range(group_count)]
            pairs = [(i, (i - turn) % group_count) for i, turn in enumerate(turns)]
            shifted.append(lax.ppermute(piece, "grp", pairs))
        return shifted

    def help_part(at, blocks):
        return pl.pallas_call(
            functools.partial(help_kernel, at),
            out_shape=block,
            in_specs=[smem, vmem, vmem],
            out_specs=vmem,
            compiler_params=shared,
            cost_estimate=pl.CostEstimate(
                flops=2 * width * tile * tile * group_size * slots,
                bytes_accessed=2 * tile * tile * group_size * slots,
                transcendentals=0,
            ),
            name="help_tiles",
        )(lent, blocks, packed)

    chunk_width = width * width // group_size

    def own_part(order, at, blocks, shifted, *states):
        out_shape = [block]
        if order < 2:
            out_shape.append(jax.ShapeDtypeStruct((group_size, width, tile), BF16))
            out_shape.append(jax.ShapeDtypeStruct((runs, width, tile), BF16))
        else:
            out_shape.append(jax.ShapeDtypeStruct((group_size, 1, chunk_width), F32))
        return pl.pallas_call(
            functools.partial(own_kernel, order, at, len(shifted)),
            out_shape=tuple(out_shape),
            in_specs=[smem, smem] + [vmem] * (len(shifted) + 2 + len(states)),
            out_specs=(vmem,) * len(out_shape),
            compiler_params=shared,
            name="own_tiles",
        )(mine, own_col, blocks, *shifted, own_tiles[0], *states)

    packed = lax.all_to_all(packed, "dev", 0, 0)
    strided_blocks = lax.all_gather(rounded, "grp", axis=0, axis_index_groups=strided)
    shifted = from_neighbours(strided_blocks)
    lent = packed[:, tile_rows + width, :slots].astype(I32)
    near = help_part(tile_rows, packed)
    first, dev_copies, grp_copies = own_part(0, tile_rows, packed, shifted, near, basis)

    def exchange(dev_copies, grp_copies):
        strided_blocks = lax.all_to_all(grp_copies, "grp", 0, 0, axis_index_groups=strided)
        group_blocks = lax.all_to_all(dev_copies, "dev", 0, 0)
        return group_blocks, from_neighbours(strided_blocks)

    group_blocks, shifted = exchange(dev_copies, grp_copies)
    near = help_part(0, group_blocks)
    second, dev_copies, grp_copies = own_part(1, 0, group_blocks, shifted, near, first, basis)
    group_blocks, shifted = exchange(dev_copies, grp_copies)
    near = help_part(0, group_blocks)
    filtered, local_gram = own_part(2, 0, group_blocks, shifted, near, second, first)

    def summed(parts, copies):
        return pl.pallas_call(
            sum_kernel,
            out_shape=jax.ShapeDtypeStruct((copies, 1, chunk_width), F32),
            in_specs=[vmem],
            out_specs=vmem,
            compiler_params=shared,
            name="sum_chunks",
        )(parts)

    parts = summed(lax.all_to_all(local_gram, "dev", 0, 0), group_count)
    parts = summed(lax.all_to_all(parts, "grp", 0, 0), group_size)
    parts = lax.all_to_all(parts, "dev", 0, 0)
    gram = pl.pallas_call(
        functools.partial(last_kernel, tile * group_size * group_count),
        out_shape=jax.ShapeDtypeStruct((width, width), F32),
        in_specs=[vmem],
        out_specs=vmem,
        compiler_params=shared,
        name="last_gram",
    )(parts)
    return filtered, gram


def solution(mesh):
    in_specs = (
        P(None, ("grp", "dev")),
        P(("grp", "dev"), None, None, None),
        P(("grp", "dev"), None),
        P(("grp", "dev"), None, None, None, None),
        P(("grp", "dev"), None, None),
        P(("grp", "dev"), None),
    )
    out_specs = (P(None, ("grp", "dev")), P())
    return jax.shard_map(
        on_device, mesh=mesh, in_specs=in_specs, out_specs=out_specs, check_vma=False
    )
```

profile of v0, /device:TPU:1, one launch (start us, length us, event | category | flops | bytes accessed | tf_op | source)
XLA Modules:
  0.0 253.9 jit_solution(13750878450286736892)
XLA Ops:
  0.6 3.5 %first_copies.1 = (bf16[32,336,128]{2,1,0:T(8,128)(2,1)}, bf16[64,128]{1,0:T(8,128)(2,1)}) custom-call(s32[2,32]{1,0:T(2,128)} %bitcast.19, s32[1,32]{1,0:T(1,128)} %count_at.1, f32[64,128]{1,0:T(8,128)} %refs_7_.1, bf16[32,256,128]{2,1,0:T(8,128)(2,1)} %bitcast.18), custom_call_target="tpu_custom_call" | custom-call | tf_op jit(solution)/shard_map/first_copies/pallas_call | solution.py:176
  4.1 0.0 copy-start.7
  4.1 17.9 %all-to-all-start = ((bf16[32,336,128]{2,1,0:T(8,128)(2,1)}), bf16[32,336,128]{2,1,0:T(8,128)(2,1)S(1)}, u32[]{:S(2)}, u32[]{:S(2)}) async-start(bf16[32,336,128]{2,1,0:T(8,128)(2,1)} %get-tuple-element.12), calls=%async_computation | async-start | bytes 5505024 | tf_op jit(solution)/shard_map/all_to_all | solution.py:239
  22.0 0.0 copy-done.7
  22.0 37.8 %all-gather = bf16[512,128]{1,0:T(8,128)(2,1)S(1)} all-gather(bf16[64,128]{1,0:T(8,128)(2,1)S(1)} %copy-done.7), channel_id=2, replica_groups={{0,128,256,384,512,640,768,896},{32,160,288,416,544,672,800,928},{64,19..., dimensions={0}, use_global_device_ids=true | all-gather | bytes 147456 | tf_op jit(solution)/shard_map/all_gather | solution.py:240
  59.9 3.0 %collective-permute-start = (bf16[8,64,128]{2,1,0:T(8,128)(2,1)S(1)}, bf16[8,64,128]{2,1,0:T(8,128)(2,1)S(1)}, u32[]{:S(2)}, u32[]{:S(2)}) collective-permute-start(bf16[8,64,128]{2,1,0:T(8,128)(2,1)S(1)} %bitcast.11), channel_id=1, source_target_pairs={{0,992},{32,0},{64,32},{96,64},{128,96},{160,128},{192,160},{224,1... | collective-permute-start | bytes 393224 | tf_op jit(solution)/shard_map/ppermute | solution.py:203
  62.8 2.8 %collective-permute-start.1 = (bf16[8,64,128]{2,1,0:T(8,128)(2,1)S(1)}, bf16[8,64,128]{2,1,0:T(8,128)(2,1)S(1)}, u32[]{:S(2)}, u32[]{:S(2)}) collective-permute-start(bf16[8,64,128]{2,1,0:T(8,128)(2,1)S(1)} %bitcast.12), channel_id=1, source_target_pairs={{0,64},{32,992},{64,128},{96,32},{128,192},{160,96},{192,256},{224... | collective-permute-start | bytes 393224 | tf_op jit(solution)/shard_map/ppermute | solution.py:203
  65.6 2.9 %collective-permute-start.2 = (bf16[8,64,128]{2,1,0:T(8,128)(2,1)S(1)}, bf16[8,64,128]{2,1,0:T(8,128)(2,1)S(1)}, u32[]{:S(2)}, u32[]{:S(2)}) collective-permute-start(bf16[8,64,128]{2,1,0:T(8,128)(2,1)S(1)} %bitcast.13), channel_id=1, source_target_pairs={{0,32},{32,64},{64,96},{96,128},{128,160},{160,192},{192,224},{224... | collective-permute-start | bytes 393224 | tf_op jit(solution)/shard_map/ppermute | solution.py:203
  68.5 0.0 all-to-all-done.blocks.packed
  68.6 0.0 copy-start
  68.6 0.0 copy-start.5
  68.6 0.0 copy-start.6
  68.6 1.6 help_tiles.3.refs_5_
  70.2 0.0 collective-permute-done.refs_1_
  70.3 0.4 collective-permute-done.1.refs_2_
  70.6 1.9 collective-permute-done.2.refs_3_
  72.6 0.0 copy-done
  72.6 0.0 copy-done.5
  72.6 0.0 copy-done.6
  72.6 1.2 own_tiles.3
  73.8 0.0 copy-start.4
  73.8 0.8 copy-done.4
  74.6 35.3 %all_to_all.40.refs_0_ = bf16[8,64,128]{2,1,0:T(8,128)(2,1)S(1)} all-to-all(bf16[8,64,128]{2,1,0:T(8,128)(2,1)S(1)} %get-tuple-element.15), channel_id=1, replica_groups={{0,128,256,384,512,640,768,896},{32,160,288,416,544,672,800,928},{64,19..., dimensions={0} | all-to-all | bytes 262144 | tf_op jit(solution)/shard_map/all_to_all | solution.py:247
  109.9 15.1 %all-to-all-start.1 = ((bf16[32,64,128]{2,1,0:T(8,128)(2,1)}), bf16[32,64,128]{2,1,0:T(8,128)(2,1)S(1)}, u32[]{:S(2)}, u32[]{:S(2)}) async-start(bf16[32,64,128]{2,1,0:T(8,128)(2,1)} %copy-done.4), calls=%async_computation.1 | async-start | bytes 1048576 | tf_op jit(solution)/shard_map/all_to_all | solution.py:248
  125.0 1.9 collective-permute-start.3
  126.9 4.3 %collective-permute-start.4 = (bf16[8,64,128]{2,1,0:T(8,128)(2,1)S(1)}, bf16[8,64,128]{2,1,0:T(8,128)(2,1)}, u32[]{:S(2)}, u32[]{:S(2)}) collective-permute-start(bf16[8,64,128]{2,1,0:T(8,128)(2,1)S(1)} %all_to_all.40.refs_0_), channel_id=1, source_target_pairs={{0,64},{32,992},{64,128},{96,32},{128,192},{160,96},{192,256},{224... | collective-permute-start | bytes 393224 | tf_op jit(solution)/shard_map/ppermute | solution.py:203
  131.2 2.1 collective-permute-start.5
  133.3 3.2 %all-to-all-done.1.blocks = bf16[32,64,128]{2,1,0:T(8,128)(2,1)S(1)} async-done(((bf16[32,64,128]{2,1,0:T(8,128)(2,1)}), bf16[32,64,128]{2,1,0:T(8,128)(2,1)S(1)}, u32[]{:S(2)}, u32[]{:S(2)}) %all-to-all-start.1) | async-done | bytes 524320 | tf_op jit(solution)/shard_map/all_to_all | solution.py:248
  136.6 0.0 copy-start.1
  136.6 1.6 help_tiles.4.refs_5_
  138.2 0.0 collective-permute-done.3.refs_1_
  138.2 0.0 collective-permute-done.4.refs_2_
  138.2 0.8 collective-permute-done.5.refs_3_
  139.0 0.0 copy-done.1
  139.0 1.7 own_tiles.4
  140.8 0.0 copy-start.3
  140.8 0.8 copy-done.3
  141.6 31.6 %all_to_all.41.refs_0_ = bf16[8,64,128]{2,1,0:T(8,128)(2,1)S(1)} all-to-all(bf16[8,64,128]{2,1,0:T(8,128)(2,1)S(1)} %get-tuple-element.18), channel_id=1, replica_groups={{0,128,256,384,512,640,768,896},{32,160,288,416,544,672,800,928},{64,19..., dimensions={0} | all-to-all | bytes 262144 | tf_op jit(solution)/shard_map/all_to_all | solution.py:247
  173.2 9.2 %all-to-all-start.3 = ((bf16[32,64,128]{2,1,0:T(8,128)(2,1)}), bf16[32,64,128]{2,1,0:T(8,128)(2,1)S(1)}, u32[]{:S(2)}, u32[]{:S(2)}) async-start(bf16[32,64,128]{2,1,0:T(8,128)(2,1)} %copy-done.3), calls=%async_computation.3 | async-start | bytes 1048576 | tf_op jit(solution)/shard_map/all_to_all | solution.py:248
  182.4 1.9 collective-permute-start.6
  184.4 4.0 %collective-permute-start.7 = (bf16[8,64,128]{2,1,0:T(8,128)(2,1)S(1)}, bf16[8,64,128]{2,1,0:T(8,128)(2,1)}, u32[]{:S(2)}, u32[]{:S(2)}) collective-permute-start(bf16[8,64,128]{2,1,0:T(8,128)(2,1)S(1)} %all_to_all.41.refs_0_), channel_id=1, source_target_pairs={{0,64},{32,992},{64,128},{96,32},{128,192},{160,96},{192,256},{224... | collective-permute-start | bytes 393224 | tf_op jit(solution)/shard_map/ppermute | solution.py:203
  188.4 2.1 collective-permute-start.8
  190.5 3.5 %all-to-all-done.3.blocks = bf16[32,64,128]{2,1,0:T(8,128)(2,1)S(1)} async-done(((bf16[32,64,128]{2,1,0:T(8,128)(2,1)}), bf16[32,64,128]{2,1,0:T(8,128)(2,1)S(1)}, u32[]{:S(2)}, u32[]{:S(2)}) %all-to-all-start.3) | async-done | bytes 524320 | tf_op jit(solution)/shard_map/all_to_all | solution.py:248
  194.0 0.0 copy-start.2
  194.0 1.6 help_tiles.5.refs_5_
  195.6 0.0 collective-permute-done.6.refs_1_
  195.6 0.0 collective-permute-done.7.refs_2_
  195.7 0.8 collective-permute-done.8.refs_3_
  196.4 0.0 copy-done.2
  196.4 2.3 own_tiles.5
  198.7 15.1 %all_to_all.42.parts = f32[32,1,128]{2,1,0:T(1,128)S(1)} all-to-all(f32[32,1,128]{2,1,0:T(1,128)S(1)} %get-tuple-element.21), channel_id=1, replica_groups=mesh['grp'=32,'dev'=32] {'dev'}, dimensions={0} | all-to-all | bytes 32768 | tf_op jit(solution)/shard_map/all_to_all | solution.py:268
  213.8 27.3 %all_to_all.43.parts = f32[32,1,128]{2,1,0:T(1,128)S(1)} all-to-all(f32[32,1,128]{2,1,0:T(1,128)S(1)} %sum_chunks.2), channel_id=1, replica_groups=mesh['grp'=32,'dev'=32] {'grp'}, dimensions={0} | all-to-all | bytes 32768 | tf_op jit(solution)/shard_map/all_to_all | solution.py:269
  241.2 12.0 %all_to_all.44.parts = f32[32,1,128]{2,1,0:T(1,128)S(1)} all-to-all(f32[32,1,128]{2,1,0:T(1,128)S(1)} %sum_chunks.3), channel_id=1, replica_groups=mesh['grp'=32,'dev'=32] {'dev'}, dimensions={0} | all-to-all | bytes 32768 | tf_op jit(solution)/shard_map/all_to_all | solution.py:270
  253.2 0.7 last_gram.1
  (3 shorter events, 0.1 us)
Async XLA Ops:
  4.1 17.9 %copy-start.7 = (bf16[64,128]{1,0:T(8,128)(2,1)S(1)}, bf16[64,128]{1,0:T(8,128)(2,1)}, u32[]{:S(2)}) copy-start(bf16[64,128]{1,0:T(8,128)(2,1)} %get-tuple-element.13) | copy-start | bytes 49156
  4.1 64.4 %all-to-all-start = ((bf16[32,336,128]{2,1,0:T(8,128)(2,1)}), bf16[32,336,128]{2,1,0:T(8,128)(2,1)S(1)}, u32[]{:S(2)}, u32[]{:S(2)}) async-start(bf16[32,336,128]{2,1,0:T(8,128)(2,1)} %get-tuple-element.12), calls=%async_computation | async-start | bytes 5505024 | tf_op jit(solution)/shard_map/all_to_all | solution.py:239
  59.9 10.4 %collective-permute-start = (bf16[8,64,128]{2,1,0:T(8,128)(2,1)S(1)}, bf16[8,64,128]{2,1,0:T(8,128)(2,1)S(1)}, u32[]{:S(2)}, u32[]{:S(2)}) collective-permute-start(bf16[8,64,128]{2,1,0:T(8,128)(2,1)S(1)} %bitcast.11), channel_id=1, source_target_pairs={{0,992},{32,0},{64,32},{96,64},{128,96},{160,128},{192,160},{224,1... | collective-permute-start | bytes 393224 | tf_op jit(solution)/shard_map/ppermute | solution.py:203
  62.8 7.8 %collective-permute-start.1 = (bf16[8,64,128]{2,1,0:T(8,128)(2,1)S(1)}, bf16[8,64,128]{2,1,0:T(8,128)(2,1)S(1)}, u32[]{:S(2)}, u32[]{:S(2)}) collective-permute-start(bf16[8,64,128]{2,1,0:T(8,128)(2,1)S(1)} %bitcast.12), channel_id=1, source_target_pairs={{0,64},{32,992},{64,128},{96,32},{128,192},{160,96},{192,256},{224... | collective-permute-start | bytes 393224 | tf_op jit(solution)/shard_map/ppermute | solution.py:203
  65.6 6.9 %collective-permute-start.2 = (bf16[8,64,128]{2,1,0:T(8,128)(2,1)S(1)}, bf16[8,64,128]{2,1,0:T(8,128)(2,1)S(1)}, u32[]{:S(2)}, u32[]{:S(2)}) collective-permute-start(bf16[8,64,128]{2,1,0:T(8,128)(2,1)S(1)} %bitcast.13), channel_id=1, source_target_pairs={{0,32},{32,64},{64,96},{96,128},{128,160},{160,192},{192,224},{224... | collective-permute-start | bytes 393224 | tf_op jit(solution)/shard_map/ppermute | solution.py:203
  68.6 4.0 %copy-start = (bf16[1,32,128,128]{3,2,1,0:T(8,128)(2,1)S(1)}, bf16[1,32,128,128]{3,2,1,0:T(8,128)(2,1)}, u32[]{:S(2)}) copy-start(bf16[1,32,128,128]{3,2,1,0:T(8,128)(2,1)} %param.7) | copy-start | bytes 3145732
  68.6 4.0 %copy-start.5 = (f32[64,128]{1,0:T(8,128)S(1)}, f32[64,128]{1,0:T(8,128)}, u32[]{:S(2)}) copy-start(f32[64,128]{1,0:T(8,128)} %refs_7_.1) | copy-start | bytes 98308
  68.6 4.0 %copy-start.6 = (s32[1,32]{1,0:T(1,128)S(1)}, s32[1,32]{1,0:T(1,128)}, u32[]{:S(2)}) copy-start(s32[1,32]{1,0:T(1,128)} %code.5) | copy-start | bytes 388
  73.8 0.8 copy-start.4
  109.9 26.6 %all-to-all-start.1 = ((bf16[32,64,128]{2,1,0:T(8,128)(2,1)}), bf16[32,64,128]{2,1,0:T(8,128)(2,1)S(1)}, u32[]{:S(2)}, u32[]{:S(2)}) async-start(bf16[32,64,128]{2,1,0:T(8,128)(2,1)} %copy-done.4), calls=%async_computation.1 | async-start | bytes 1048576 | tf_op jit(solution)/shard_map/all_to_all | solution.py:248
  125.0 13.2 %collective-permute-start.3 = (bf16[8,64,128]{2,1,0:T(8,128)(2,1)S(1)}, bf16[8,64,128]{2,1,0:T(8,128)(2,1)}, u32[]{:S(2)}, u32[]{:S(2)}) collective-permute-start(bf16[8,64,128]{2,1,0:T(8,128)(2,1)S(1)} %all_to_all.40.refs_0_), channel_id=1, source_target_pairs={{0,992},{32,0},{64,32},{96,64},{128,96},{160,128},{192,160},{224,1... | collective-permute-start | bytes 393224 | tf_op jit(solution)/shard_map/ppermute | solution.py:203
  126.9 11.3 %collective-permute-start.4 = (bf16[8,64,128]{2,1,0:T(8,128)(2,1)S(1)}, bf16[8,64,128]{2,1,0:T(8,128)(2,1)}, u32[]{:S(2)}, u32[]{:S(2)}) collective-permute-start(bf16[8,64,128]{2,1,0:T(8,128)(2,1)S(1)} %all_to_all.40.refs_0_), channel_id=1, source_target_pairs={{0,64},{32,992},{64,128},{96,32},{128,192},{160,96},{192,256},{224... | collective-permute-start | bytes 393224 | tf_op jit(solution)/shard_map/ppermute | solution.py:203
  131.2 7.8 %collective-permute-start.5 = (bf16[8,64,128]{2,1,0:T(8,128)(2,1)S(1)}, bf16[8,64,128]{2,1,0:T(8,128)(2,1)}, u32[]{:S(2)}, u32[]{:S(2)}) collective-permute-start(bf16[8,64,128]{2,1,0:T(8,128)(2,1)S(1)} %all_to_all.40.refs_0_), channel_id=1, source_target_pairs={{0,32},{32,64},{64,96},{96,128},{128,160},{160,192},{192,224},{224... | collective-permute-start | bytes 393224 | tf_op jit(solution)/shard_map/ppermute | solution.py:203
  136.6 2.5 copy-start.1
  140.8 0.8 copy-start.3
  173.2 20.8 %all-to-all-start.3 = ((bf16[32,64,128]{2,1,0:T(8,128)(2,1)}), bf16[32,64,128]{2,1,0:T(8,128)(2,1)S(1)}, u32[]{:S(2)}, u32[]{:S(2)}) async-start(bf16[32,64,128]{2,1,0:T(8,128)(2,1)} %copy-done.3), calls=%async_computation.3 | async-start | bytes 1048576 | tf_op jit(solution)/shard_map/all_to_all | solution.py:248
  182.4 13.2 %collective-permute-start.6 = (bf16[8,64,128]{2,1,0:T(8,128)(2,1)S(1)}, bf16[8,64,128]{2,1,0:T(8,128)(2,1)}, u32[]{:S(2)}, u32[]{:S(2)}) collective-permute-start(bf16[8,64,128]{2,1,0:T(8,128)(2,1)S(1)} %all_to_all.41.refs_0_), channel_id=1, source_target_pairs={{0,992},{32,0},{64,32},{96,64},{128,96},{160,128},{192,160},{224,1... | collective-permute-start | bytes 393224 | tf_op jit(solution)/shard_map/ppermute | solution.py:203
  184.4 11.3 %collective-permute-start.7 = (bf16[8,64,128]{2,1,0:T(8,128)(2,1)S(1)}, bf16[8,64,128]{2,1,0:T(8,128)(2,1)}, u32[]{:S(2)}, u32[]{:S(2)}) collective-permute-start(bf16[8,64,128]{2,1,0:T(8,128)(2,1)S(1)} %all_to_all.41.refs_0_), channel_id=1, source_target_pairs={{0,64},{32,992},{64,128},{96,32},{128,192},{160,96},{192,256},{224... | collective-permute-start | bytes 393224 | tf_op jit(solution)/shard_map/ppermute | solution.py:203
  188.4 8.1 %collective-permute-start.8 = (bf16[8,64,128]{2,1,0:T(8,128)(2,1)S(1)}, bf16[8,64,128]{2,1,0:T(8,128)(2,1)}, u32[]{:S(2)}, u32[]{:S(2)}) collective-permute-start(bf16[8,64,128]{2,1,0:T(8,128)(2,1)S(1)} %all_to_all.41.refs_0_), channel_id=1, source_target_pairs={{0,32},{32,64},{64,96},{96,128},{128,160},{160,192},{192,224},{224... | collective-permute-start | bytes 393224 | tf_op jit(solution)/shard_map/ppermute | solution.py:203
  194.0 2.4 copy-start.2
where the time goes:
time: 255 us; the launch traced here: 254 us
  blocking collectives  159 us (62%)
  starting transfers between devices  67.2 us (26%)
  Pallas kernels  14.3 us (6%)
  waiting for transfers between devices  10.6 us (4%)
    all_to_all x2, blocking collectives, exchange(): lax.all_to_all(grp_copies, 'grp', 0, 0, axis_index_groups=strided)  67 us
    all_gather x1, blocking collectives, on_device(): lax.all_gather(rounded, 'grp', axis=0, axis_index_groups=strided)  37.8 us
    all_to_all x1, blocking collectives, on_device(): parts = summed(lax.all_to_all(parts, 'grp', 0, 0), group_size)  27.3 us
    ppermute x9, starting transfers between devices, from_neighbours(): shifted.append(lax.ppermute(piece, 'grp', pairs))  25 us
    all_to_all x2, starting transfers between devices, exchange(): group_blocks = lax.all_to_all(dev_copies, 'dev', 0, 0)  24.3 us
    all_to_all x1, starting transfers between devices, on_device(): packed = lax.all_to_all(packed, 'dev', 0, 0)  17.9 us
    all_to_all x1, blocking collectives, on_device(): parts = summed(lax.all_to_all(local_gram, 'dev', 0, 0), group_count)  15.1 us
    all_to_all x1, blocking collectives, on_device(): parts = lax.all_to_all(parts, 'dev', 0, 0)  12 us
  transfers between devices with their start and end apart: 12, of which 6 were waited for; matrix products, arithmetic and copies ran while one was open for 0% of the time, Pallas kernels for 2%

commit v1 on v0

--- a/solution.py
+++ b/solution.py
@@ -8,7 +8,8 @@
 from jax.sharding import PartitionSpec as P
 
 STRIDE = 4
-SHIFTS = {2: (1, -1), 4: (1, 2, -1)}[STRIDE]
+SHIFTS = (2, 1, -1)
+TURNS = (0, *(shift % STRIDE for shift in SHIFTS))
 UNROLL = 8
 HEADER = 16
 CUTS = 8
@@ -112,8 +113,8 @@
         turn = lax.rem(far - mine[0] + STRIDE * total_runs, STRIDE)
         run = lax.div(far, STRIDE)
         found = blocks[jnp.where(live, 0, c), pl.ds(at, rows)]
-        for i in range(STRIDE):
-            found = jnp.where(live & (turn == i), parts[i][run], found)
+        for i, part in zip(TURNS, parts):
+            found = jnp.where(live & (turn == i), part[run], found)
         return found
 
     product = near[...]
@@ -193,15 +194,12 @@
     )(help_col[0].T, help_count, basis, help_tiles[0].reshape(group_size, tile_rows, tile))
 
     def from_neighbours(strided_blocks):
-        shifted = [strided_blocks]
-        for n, shift in enumerate(SHIFTS):
-            piece = strided_blocks
-            if STRIDE == 2:
-                piece = strided_blocks[n * (runs // 2) : (n + 1) * (runs // 2)]
+        shifted = {0: strided_blocks}
+        for shift in SHIFTS:
             turns = [shift if i % 2 or abs(shift) == 1 else -shift for i in range(group_count)]
             pairs = [(i, (i - turn) % group_count) for i, turn in enumerate(turns)]
-            shifted.append(lax.ppermute(piece, "grp", pairs))
-        return shifted
+            shifted[shift % STRIDE] = lax.ppermute(strided_blocks, "grp", pairs)
+        return [shifted[turn] for turn in TURNS]
 
     def help_part(at, blocks):
         return pl.pallas_call(

time: 255 us -> 255 us (level)
  starting transfers between devices: 67.2 us -> 70.3 us
    all_to_all x2, blocking collectives: 67 us -> 64 us  [exchange(): lax.all_to_all(grp_copies, 'grp', 0, 0, axis_index_groups=strided)]
  transfers between devices with their start and end apart: 12 -> 12, of which waited for: 6 -> 4; matrix products, arithmetic and copies ran while one was open for 0% -> 0% of each run, Pallas kernels for 2% -> 2%
where the time goes in v1:
time: 255 us; the launch traced here: 254 us
  blocking collectives  157 us (62%)
  starting transfers between devices  70.3 us (28%)
  Pallas kernels  14.3 us (6%)
  waiting for transfers between devices  9.41 us (4%)
    all_to_all x2, blocking collectives, exchange(): lax.all_to_all(grp_copies, 'grp', 0, 0, axis_index_groups=strided)  64 us
    all_gather x1, blocking collectives, on_device(): lax.all_gather(rounded, 'grp', axis=0, axis_index_groups=strided)  37.8 us
    all_to_all x1, blocking collectives, on_device(): parts = summed(lax.all_to_all(parts, 'grp', 0, 0), group_size)  28.5 us
    ppermute x9, starting transfers between devices, from_neighbours(): shifted[shift % STRIDE] = lax.ppermute(strided_blocks, 'grp', pairs)  26.5 us
    all_to_all x2, starting transfers between devices, exchange(): group_blocks = lax.all_to_all(dev_copies, 'dev', 0, 0)  25.8 us
    all_to_all x1, starting transfers between devices, on_device(): packed = lax.all_to_all(packed, 'dev', 0, 0)  17.9 us
    all_to_all x1, blocking collectives, on_device(): parts = summed(lax.all_to_all(local_gram, 'dev', 0, 0), group_count)  15.1 us
    all_to_all x1, blocking collectives, on_device(): parts = lax.all_to_all(parts, 'dev', 0, 0)  12 us
  transfers between devices with their start and end apart: 12, of which 4 were waited for; matrix products, arithmetic and copies ran while one was open for 0% of the time, Pallas kernels for 2%

profile of v1, /device:TPU:1, one launch (start us, length us, event | category | flops | bytes accessed | tf_op | source)
XLA Modules:
  0.0 254.0 jit_solution(8507127247950680141)
XLA Ops:
  0.6 3.5 %first_copies.1 = (bf16[32,336,128]{2,1,0:T(8,128)(2,1)}, bf16[64,128]{1,0:T(8,128)(2,1)}) custom-call(s32[2,32]{1,0:T(2,128)} %bitcast.19, s32[1,32]{1,0:T(1,128)} %count_at.1, f32[64,128]{1,0:T(8,128)} %refs_7_.1, bf16[32,256,128]{2,1,0:T(8,128)(2,1)} %bitcast.18), custom_call_target="tpu_custom_call" | custom-call | tf_op jit(solution)/shard_map/first_copies/pallas_call | solution.py:177
  4.1 0.0 copy-start.7
  4.1 17.9 %all-to-all-start = ((bf16[32,336,128]{2,1,0:T(8,128)(2,1)}), bf16[32,336,128]{2,1,0:T(8,128)(2,1)S(1)}, u32[]{:S(2)}, u32[]{:S(2)}) async-start(bf16[32,336,128]{2,1,0:T(8,128)(2,1)} %get-tuple-element.12), calls=%async_computation | async-start | bytes 5505024 | tf_op jit(solution)/shard_map/all_to_all | solution.py:237
  22.0 0.0 copy-done.7
  22.0 37.8 %all-gather = bf16[512,128]{1,0:T(8,128)(2,1)S(1)} all-gather(bf16[64,128]{1,0:T(8,128)(2,1)S(1)} %copy-done.7), channel_id=2, replica_groups={{0,128,256,384,512,640,768,896},{32,160,288,416,544,672,800,928},{64,19..., dimensions={0}, use_global_device_ids=true | all-gather | bytes 147456 | tf_op jit(solution)/shard_map/all_gather | solution.py:238
  59.9 3.1 %collective-permute-start = (bf16[8,64,128]{2,1,0:T(8,128)(2,1)S(1)}, bf16[8,64,128]{2,1,0:T(8,128)(2,1)S(1)}, u32[]{:S(2)}, u32[]{:S(2)}) collective-permute-start(bf16[8,64,128]{2,1,0:T(8,128)(2,1)S(1)} %bitcast.11), channel_id=1, source_target_pairs={{0,64},{32,992},{64,128},{96,32},{128,192},{160,96},{192,256},{224... | collective-permute-start | bytes 393224 | tf_op jit(solution)/shard_map/ppermute | solution.py:201
  62.9 3.0 %collective-permute-start.1 = (bf16[8,64,128]{2,1,0:T(8,128)(2,1)S(1)}, bf16[8,64,128]{2,1,0:T(8,128)(2,1)S(1)}, u32[]{:S(2)}, u32[]{:S(2)}) collective-permute-start(bf16[8,64,128]{2,1,0:T(8,128)(2,1)S(1)} %bitcast.12), channel_id=1, source_target_pairs={{0,992},{32,0},{64,32},{96,64},{128,96},{160,128},{192,160},{224,1... | collective-permute-start | bytes 393224 | tf_op jit(solution)/shard_map/ppermute | solution.py:201
  66.0 2.3 collective-permute-start.2
  68.2 0.0 all-to-all-done.blocks.packed
  68.3 0.0 copy-start
  68.3 0.0 copy-start.5
  68.3 0.0 copy-start.6
  68.3 1.6 help_tiles.3.refs_5_
  69.9 0.0 collective-permute-done.refs_1_
  70.0 0.0 collective-permute-done.1.refs_2_
  70.0 3.9 %collective-permute-done.2.refs_3_ = bf16[8,64,128]{2,1,0:T(8,128)(2,1)S(1)} collective-permute-done((bf16[8,64,128]{2,1,0:T(8,128)(2,1)S(1)}, bf16[8,64,128]{2,1,0:T(8,128)(2,1)S(1)}, u32[]{:S(2)}, u32[]{:S(2)}) %collective-permute-start.2) | collective-permute-done | bytes 131104 | tf_op jit(solution)/shard_map/ppermute | solution.py:201
  73.9 0.0 copy-done
  73.9 0.0 copy-done.5
  73.9 0.0 copy-done.6
  73.9 1.2 own_tiles.3
  75.1 0.0 copy-start.4
  75.1 0.8 copy-done.4
  75.9 35.0 %all_to_all.40.refs_0_ = bf16[8,64,128]{2,1,0:T(8,128)(2,1)S(1)} all-to-all(bf16[8,64,128]{2,1,0:T(8,128)(2,1)S(1)} %get-tuple-element.15), channel_id=1, replica_groups={{0,128,256,384,512,640,768,896},{32,160,288,416,544,672,800,928},{64,19..., dimensions={0} | all-to-all | bytes 262144 | tf_op jit(solution)/shard_map/all_to_all | solution.py:245
  110.9 14.0 %all-to-all-start.1 = ((bf16[32,64,128]{2,1,0:T(8,128)(2,1)}), bf16[32,64,128]{2,1,0:T(8,128)(2,1)S(1)}, u32[]{:S(2)}, u32[]{:S(2)}) async-start(bf16[32,64,128]{2,1,0:T(8,128)(2,1)} %copy-done.4), calls=%async_computation.1 | async-start | bytes 1048576 | tf_op jit(solution)/shard_map/all_to_all | solution.py:246
  124.9 4.1 %collective-permute-start.3 = (bf16[8,64,128]{2,1,0:T(8,128)(2,1)S(1)}, bf16[8,64,128]{2,1,0:T(8,128)(2,1)}, u32[]{:S(2)}, u32[]{:S(2)}) collective-permute-start(bf16[8,64,128]{2,1,0:T(8,128)(2,1)S(1)} %all_to_all.40.refs_0_), channel_id=1, source_target_pairs={{0,64},{32,992},{64,128},{96,32},{128,192},{160,96},{192,256},{224... | collective-permute-start | bytes 393224 | tf_op jit(solution)/shard_map/ppermute | solution.py:201
  129.0 1.9 collective-permute-start.4
  130.9 3.4 %collective-permute-start.5 = (bf16[8,64,128]{2,1,0:T(8,128)(2,1)S(1)}, bf16[8,64,128]{2,1,0:T(8,128)(2,1)}, u32[]{:S(2)}, u32[]{:S(2)}) collective-permute-start(bf16[8,64,128]{2,1,0:T(8,128)(2,1)S(1)} %all_to_all.40.refs_0_), channel_id=1, source_target_pairs={{0,32},{32,64},{64,96},{96,128},{128,160},{160,192},{192,224},{224... | collective-permute-start | bytes 393224 | tf_op jit(solution)/shard_map/ppermute | solution.py:201
  134.3 2.1 all-to-all-done.1.blocks
  136.4 0.0 copy-start.1
  136.4 1.6 help_tiles.4.refs_5_
  138.1 0.0 collective-permute-done.3.refs_1_
  138.1 0.0 collective-permute-done.4.refs_2_
  138.1 0.6 collective-permute-done.5.refs_3_
  138.7 0.0 copy-done.1
  138.7 1.7 own_tiles.4
  140.4 0.0 copy-start.3
  140.4 0.8 copy-done.3
  141.2 29.0 %all_to_all.41.refs_0_ = bf16[8,64,128]{2,1,0:T(8,128)(2,1)S(1)} all-to-all(bf16[8,64,128]{2,1,0:T(8,128)(2,1)S(1)} %get-tuple-element.18), channel_id=1, replica_groups={{0,128,256,384,512,640,768,896},{32,160,288,416,544,672,800,928},{64,19..., dimensions={0} | all-to-all | bytes 262144 | tf_op jit(solution)/shard_map/all_to_all | solution.py:245
  170.2 11.9 %all-to-all-start.3 = ((bf16[32,64,128]{2,1,0:T(8,128)(2,1)}), bf16[32,64,128]{2,1,0:T(8,128)(2,1)S(1)}, u32[]{:S(2)}, u32[]{:S(2)}) async-start(bf16[32,64,128]{2,1,0:T(8,128)(2,1)} %copy-done.3), calls=%async_computation.3 | async-start | bytes 1048576 | tf_op jit(solution)/shard_map/all_to_all | solution.py:246
  182.1 3.5 %collective-permute-start.6 = (bf16[8,64,128]{2,1,0:T(8,128)(2,1)S(1)}, bf16[8,64,128]{2,1,0:T(8,128)(2,1)}, u32[]{:S(2)}, u32[]{:S(2)}) collective-permute-start(bf16[8,64,128]{2,1,0:T(8,128)(2,1)S(1)} %all_to_all.41.refs_0_), channel_id=1, source_target_pairs={{0,64},{32,992},{64,128},{96,32},{128,192},{160,96},{192,256},{224... | collective-permute-start | bytes 393224 | tf_op jit(solution)/shard_map/ppermute | solution.py:201
  185.6 1.9 collective-permute-start.7
  187.5 3.4 %collective-permute-start.8 = (bf16[8,64,128]{2,1,0:T(8,128)(2,1)S(1)}, bf16[8,64,128]{2,1,0:T(8,128)(2,1)}, u32[]{:S(2)}, u32[]{:S(2)}) collective-permute-start(bf16[8,64,128]{2,1,0:T(8,128)(2,1)S(1)} %all_to_all.41.refs_0_), channel_id=1, source_target_pairs={{0,32},{32,64},{64,96},{96,128},{128,160},{160,192},{192,224},{224... | collective-permute-start | bytes 393224 | tf_op jit(solution)/shard_map/ppermute | solution.py:201
  190.9 2.7 %all-to-all-done.3.blocks = bf16[32,64,128]{2,1,0:T(8,128)(2,1)S(1)} async-done(((bf16[32,64,128]{2,1,0:T(8,128)(2,1)}), bf16[32,64,128]{2,1,0:T(8,128)(2,1)S(1)}, u32[]{:S(2)}, u32[]{:S(2)}) %all-to-all-start.3) | async-done | bytes 524320 | tf_op jit(solution)/shard_map/all_to_all | solution.py:246
  193.6 0.0 copy-start.2
  193.6 1.6 help_tiles.5.refs_5_
  195.3 0.0 collective-permute-done.6.refs_1_
  195.3 0.0 collective-permute-done.7.refs_2_
  195.3 0.0 collective-permute-done.8.refs_3_
  195.3 0.0 copy-done.2
  195.3 2.3 own_tiles.5
  197.6 15.1 %all_to_all.42.parts = f32[32,1,128]{2,1,0:T(1,128)S(1)} all-to-all(f32[32,1,128]{2,1,0:T(1,128)S(1)} %get-tuple-element.21), channel_id=1, replica_groups=mesh['grp'=32,'dev'=32] {'dev'}, dimensions={0} | all-to-all | bytes 32768 | tf_op jit(solution)/shard_map/all_to_all | solution.py:266
  212.7 28.5 %all_to_all.43.parts = f32[32,1,128]{2,1,0:T(1,128)S(1)} all-to-all(f32[32,1,128]{2,1,0:T(1,128)S(1)} %sum_chunks.2), channel_id=1, replica_groups=mesh['grp'=32,'dev'=32] {'grp'}, dimensions={0} | all-to-all | bytes 32768 | tf_op jit(solution)/shard_map/all_to_all | solution.py:267
  241.3 12.0 %all_to_all.44.parts = f32[32,1,128]{2,1,0:T(1,128)S(1)} all-to-all(f32[32,1,128]{2,1,0:T(1,128)S(1)} %sum_chunks.3), channel_id=1, replica_groups=mesh['grp'=32,'dev'=32] {'dev'}, dimensions={0} | all-to-all | bytes 32768 | tf_op jit(solution)/shard_map/all_to_all | solution.py:268
  253.3 0.7 last_gram.1
  (3 shorter events, 0.1 us)
Async XLA Ops:
  4.1 17.9 %copy-start.7 = (bf16[64,128]{1,0:T(8,128)(2,1)S(1)}, bf16[64,128]{1,0:T(8,128)(2,1)}, u32[]{:S(2)}) copy-start(bf16[64,128]{1,0:T(8,128)(2,1)} %get-tuple-element.13) | copy-start | bytes 49156
  4.1 64.1 %all-to-all-start = ((bf16[32,336,128]{2,1,0:T(8,128)(2,1)}), bf16[32,336,128]{2,1,0:T(8,128)(2,1)S(1)}, u32[]{:S(2)}, u32[]{:S(2)}) async-start(bf16[32,336,128]{2,1,0:T(8,128)(2,1)} %get-tuple-element.12), calls=%async_computation | async-start | bytes 5505024 | tf_op jit(solution)/shard_map/all_to_all | solution.py:237
  59.9 10.1 %collective-permute-start = (bf16[8,64,128]{2,1,0:T(8,128)(2,1)S(1)}, bf16[8,64,128]{2,1,0:T(8,128)(2,1)S(1)}, u32[]{:S(2)}, u32[]{:S(2)}) collective-permute-start(bf16[8,64,128]{2,1,0:T(8,128)(2,1)S(1)} %bitcast.11), channel_id=1, source_target_pairs={{0,64},{32,992},{64,128},{96,32},{128,192},{160,96},{192,256},{224... | collective-permute-start | bytes 393224 | tf_op jit(solution)/shard_map/ppermute | solution.py:201
  62.9 7.0 %collective-permute-start.1 = (bf16[8,64,128]{2,1,0:T(8,128)(2,1)S(1)}, bf16[8,64,128]{2,1,0:T(8,128)(2,1)S(1)}, u32[]{:S(2)}, u32[]{:S(2)}) collective-permute-start(bf16[8,64,128]{2,1,0:T(8,128)(2,1)S(1)} %bitcast.12), channel_id=1, source_target_pairs={{0,992},{32,0},{64,32},{96,64},{128,96},{160,128},{192,160},{224,1... | collective-permute-start | bytes 393224 | tf_op jit(solution)/shard_map/ppermute | solution.py:201
  66.0 7.9 %collective-permute-start.2 = (bf16[8,64,128]{2,1,0:T(8,128)(2,1)S(1)}, bf16[8,64,128]{2,1,0:T(8,128)(2,1)S(1)}, u32[]{:S(2)}, u32[]{:S(2)}) collective-permute-start(bf16[8,64,128]{2,1,0:T(8,128)(2,1)S(1)} %bitcast.13), channel_id=1, source_target_pairs={{0,32},{32,64},{64,96},{96,128},{128,160},{160,192},{192,224},{224... | collective-permute-start | bytes 393224 | tf_op jit(solution)/shard_map/ppermute | solution.py:201
  68.3 5.6 %copy-start = (bf16[1,32,128,128]{3,2,1,0:T(8,128)(2,1)S(1)}, bf16[1,32,128,128]{3,2,1,0:T(8,128)(2,1)}, u32[]{:S(2)}) copy-start(bf16[1,32,128,128]{3,2,1,0:T(8,128)(2,1)} %param.7) | copy-start | bytes 3145732
  68.3 5.6 %copy-start.5 = (f32[64,128]{1,0:T(8,128)S(1)}, f32[64,128]{1,0:T(8,128)}, u32[]{:S(2)}) copy-start(f32[64,128]{1,0:T(8,128)} %refs_7_.1) | copy-start | bytes 98308
  68.3 5.6 %copy-start.6 = (s32[1,32]{1,0:T(1,128)S(1)}, s32[1,32]{1,0:T(1,128)}, u32[]{:S(2)}) copy-start(s32[1,32]{1,0:T(1,128)} %code.5) | copy-start | bytes 388
  75.1 0.8 copy-start.4
  110.9 25.5 %all-to-all-start.1 = ((bf16[32,64,128]{2,1,0:T(8,128)(2,1)}), bf16[32,64,128]{2,1,0:T(8,128)(2,1)S(1)}, u32[]{:S(2)}, u32[]{:S(2)}) async-start(bf16[32,64,128]{2,1,0:T(8,128)(2,1)} %copy-done.4), calls=%async_computation.1 | async-start | bytes 1048576 | tf_op jit(solution)/shard_map/all_to_all | solution.py:246
  124.9 13.2 %collective-permute-start.3 = (bf16[8,64,128]{2,1,0:T(8,128)(2,1)S(1)}, bf16[8,64,128]{2,1,0:T(8,128)(2,1)}, u32[]{:S(2)}, u32[]{:S(2)}) collective-permute-start(bf16[8,64,128]{2,1,0:T(8,128)(2,1)S(1)} %all_to_all.40.refs_0_), channel_id=1, source_target_pairs={{0,64},{32,992},{64,128},{96,32},{128,192},{160,96},{192,256},{224... | collective-permute-start | bytes 393224 | tf_op jit(solution)/shard_map/ppermute | solution.py:201
  129.0 9.1 %collective-permute-start.4 = (bf16[8,64,128]{2,1,0:T(8,128)(2,1)S(1)}, bf16[8,64,128]{2,1,0:T(8,128)(2,1)}, u32[]{:S(2)}, u32[]{:S(2)}) collective-permute-start(bf16[8,64,128]{2,1,0:T(8,128)(2,1)S(1)} %all_to_all.40.refs_0_), channel_id=1, source_target_pairs={{0,992},{32,0},{64,32},{96,64},{128,96},{160,128},{192,160},{224,1... | collective-permute-start | bytes 393224 | tf_op jit(solution)/shard_map/ppermute | solution.py:201
  130.9 7.8 %collective-permute-start.5 = (bf16[8,64,128]{2,1,0:T(8,128)(2,1)S(1)}, bf16[8,64,128]{2,1,0:T(8,128)(2,1)}, u32[]{:S(2)}, u32[]{:S(2)}) collective-permute-start(bf16[8,64,128]{2,1,0:T(8,128)(2,1)S(1)} %all_to_all.40.refs_0_), channel_id=1, source_target_pairs={{0,32},{32,64},{64,96},{96,128},{128,160},{160,192},{192,224},{224... | collective-permute-start | bytes 393224 | tf_op jit(solution)/shard_map/ppermute | solution.py:201
  136.4 2.2 copy-start.1
  140.4 0.8 copy-start.3
  170.2 23.5 %all-to-all-start.3 = ((bf16[32,64,128]{2,1,0:T(8,128)(2,1)}), bf16[32,64,128]{2,1,0:T(8,128)(2,1)S(1)}, u32[]{:S(2)}, u32[]{:S(2)}) async-start(bf16[32,64,128]{2,1,0:T(8,128)(2,1)} %copy-done.3), calls=%async_computation.3 | async-start | bytes 1048576 | tf_op jit(solution)/shard_map/all_to_all | solution.py:246
  182.1 13.2 %collective-permute-start.6 = (bf16[8,64,128]{2,1,0:T(8,128)(2,1)S(1)}, bf16[8,64,128]{2,1,0:T(8,128)(2,1)}, u32[]{:S(2)}, u32[]{:S(2)}) collective-permute-start(bf16[8,64,128]{2,1,0:T(8,128)(2,1)S(1)} %all_to_all.41.refs_0_), channel_id=1, source_target_pairs={{0,64},{32,992},{64,128},{96,32},{128,192},{160,96},{192,256},{224... | collective-permute-start | bytes 393224 | tf_op jit(solution)/shard_map/ppermute | solution.py:201
  185.6 9.7 %collective-permute-start.7 = (bf16[8,64,128]{2,1,0:T(8,128)(2,1)S(1)}, bf16[8,64,128]{2,1,0:T(8,128)(2,1)}, u32[]{:S(2)}, u32[]{:S(2)}) collective-permute-start(bf16[8,64,128]{2,1,0:T(8,128)(2,1)S(1)} %all_to_all.41.refs_0_), channel_id=1, source_target_pairs={{0,992},{32,0},{64,32},{96,64},{128,96},{160,128},{192,160},{224,1... | collective-permute-start | bytes 393224 | tf_op jit(solution)/shard_map/ppermute | solution.py:201
  187.5 7.8 %collective-permute-start.8 = (bf16[8,64,128]{2,1,0:T(8,128)(2,1)S(1)}, bf16[8,64,128]{2,1,0:T(8,128)(2,1)}, u32[]{:S(2)}, u32[]{:S(2)}) collective-permute-start(bf16[8,64,128]{2,1,0:T(8,128)(2,1)S(1)} %all_to_all.41.refs_0_), channel_id=1, source_target_pairs={{0,32},{32,64},{64,96},{96,128},{128,160},{160,192},{192,224},{224... | collective-permute-start | bytes 393224 | tf_op jit(solution)/shard_map/ppermute | solution.py:201
  193.6 1.7 copy-start.2
